TPU v7x, 256 devices: a whole 4x4x8 slice. The times are simulated.
256 devices in a mesh: fsdp: 16 (over z, core), slab: 8 (over y, x_lo), rep: 2 (over x_hi).
Axes of the slice: x: 4 (x_hi: 2, x_lo: 2; x = x_hi * 2 + x_lo), y: 4, z: 8, core: 2. Of those that a mesh axis runs over, the one named last changes fastest.
Arguments:
- inputs: bfloat16 [32, 32, 8, 8, 256], P(('fsdp', 'rep'), 'slab'), may hold values from -6 to 6
- weights: bfloat16 [256, 27, 256], P('fsdp'), may hold values from -0.078125 to 0.078125
- upstream: bfloat16 [32, 32, 8, 8, 256], P(('fsdp', 'rep'), 'slab'), may hold values from -6 to 6
Outputs:
- activated: bfloat16 [32, 32, 8, 8, 256], P(('fsdp', 'rep'), 'slab')
- input_grad: bfloat16 [32, 32, 8, 8, 256], P(('fsdp', 'rep'), 'slab')
- weight_grad: float32 [256, 27, 256], P('fsdp')
All inputs are finite; a program needn't handle non-finite values.
Results may differ from a plain program's by a relative error of at most 0.0049.
Values may be sent and summed in bfloat16 or wider, within the bound.
No kernel may reach another device: no remote copies, remote signals or barrier semaphores. Data moves between devices by JAX's collectives and lax.ppermute only.
A program may use at most 256 MiB of HBM per device.

v0:
```python
import jax
import jax.numpy as jnp
from jax import lax
from jax.sharding import PartitionSpec as P


def padded_2(cells, sides, width):
    for axis, dim in sides:
        count = lax.axis_size(axis)
        ends = count - 1
        head = lax.slice_in_dim(cells, 0, width, axis=dim)
        tail = lax.slice_in_dim(cells, cells.shape[dim] - width, cells.shape[dim], axis=dim)
        cells = jnp.concatenate(
            [
                lax.ppermute(tail, axis, [(i, (i + 1) % count) for i in range(ends)]),
                cells,
                lax.ppermute(head, axis, [((i + 1) % count, i) for i in range(ends)]),
            ],
            axis=dim,
        )
    return cells


def silu_slope(preact):
    logistic = jax.nn.sigmoid(preact)
    return logistic * (1.0 + preact * (1.0 - logistic))


def pad_cross(field):
    return jnp.pad(field, ((0, 0), (0, 0), (1, 1), (1, 1), (0, 0)))


def grad_rim(field):
    return pad_cross(padded_2(field, (("slab", 1),), 1))


def tap_list():
    return [
        (along_x, along_y, along_z)
        for along_x in range(3)
        for along_y in range(3)
        for along_z in range(3)
    ]


def forward_rows(padded, weight_rows):
    planes = padded.shape[1] - 2
    height = padded.shape[2] - 2
    breadth = padded.shape[3] - 2
    total = None
    for index, (along_x, along_y, along_z) in enumerate(tap_list()):
        window = padded[
            :,
            along_x : along_x + planes,
            along_y : along_y + height,
            along_z : along_z + breadth,
            :,
        ]
        term = jnp.einsum(
            "bxyzi,oi->bxyzo", window, weight_rows[:, index, :], preferred_element_type=jnp.float32
        )
        total = term if total is None else total + term
    return total


def backward_rows(grads_pad, weight_rows):
    planes = grads_pad.shape[1] - 2
    height = grads_pad.shape[2] - 2
    breadth = grads_pad.shape[3] - 2
    total = None
    for index, (along_x, along_y, along_z) in enumerate(tap_list()):
        grad_window = grads_pad[
            :,
            2 - along_x : 2 - along_x + planes,
            2 - along_y : 2 - along_y + height,
            2 - along_z : 2 - along_z + breadth,
            :,
        ]
        term = jnp.einsum(
            "bxyzo,oi->bxyzi",
            grad_window,
            weight_rows[:, index, :],
            preferred_element_type=jnp.float32,
        )
        total = term if total is None else total + term
    return total


def weight_terms(grads, padded, factor):
    planes = grads.shape[1]
    height = grads.shape[2]
    breadth = grads.shape[3]
    stacked = []
    for along_x, along_y, along_z in tap_list():
        window = padded[
            :,
            along_x : along_x + planes,
            along_y : along_y + height,
            along_z : along_z + breadth,
            :,
        ]
        stacked.append(
            jnp.einsum("bxyzo,bxyzi->oi", grads, window, preferred_element_type=jnp.float32)
        )
    return jnp.stack(stacked, axis=1) * factor


def local(inputs, weights, upstream):
    samples = inputs.shape[0]
    planes = inputs.shape[1]
    height = inputs.shape[2]
    breadth = inputs.shape[3]
    total_cells = (
        samples
        * lax.axis_size("fsdp")
        * lax.axis_size("rep")
        * planes
        * lax.axis_size("slab")
        * height
        * breadth
    )
    factor = float(total_cells) ** (-0.5)
    inputs_halo = padded_2(inputs, (("slab", 1),), 1)
    inputs_pad = pad_cross(inputs_halo)
    whole = lax.all_gather(weights, "fsdp", axis=0, tiled=True)
    preact = forward_rows(inputs_pad, whole)
    activated = jax.nn.silu(preact).astype(jnp.bfloat16)
    grad_pre = (upstream.astype(jnp.float32) * silu_slope(preact)).astype(jnp.bfloat16)
    grads_pad = grad_rim(grad_pre)
    input_grad = backward_rows(grads_pad, whole).astype(jnp.bfloat16)
    terms = weight_terms(grad_pre, inputs_pad, factor)
    shard = lax.psum_scatter(terms, "fsdp", scatter_dimension=0, tiled=True)
    weight_grad = lax.psum(shard, ("slab", "rep"))
    return (activated, input_grad, weight_grad)


def solution(mesh):
    placed = (
        P(("fsdp", "rep"), "slab", None, None, None),
        P("fsdp", None, None),
        P(("fsdp", "rep"), "slab", None, None, None),
    )
    return jax.shard_map(
        local,
        mesh=mesh,
        in_specs=placed,
        out_specs=(
            P(("fsdp", "rep"), "slab", None, None, None),
            P(("fsdp", "rep"), "slab", None, None, None),
            P("fsdp", None, None),
        ),
        check_vma=False,
    )
```

profile of v0, /device:TPU:32, one launch (start us, length us, event | category | flops | bytes accessed | tf_op | source)
XLA Modules:
  0.0 247.4 jit_solution(10040391627877063961)
XLA Ops:
  8.7 3.4 %collective-permute-start = (bf16[1,1,8,8,256]{4,3,2,1,0:T(8,128)(2,1)S(1)}, bf16[1,1,8,8,256]{4,3,2,1,0:T(8,128)(2,1)S(1)}, u32[]{:S(2)}, u32[]{:S(2)}) collective-permute-start(bf16[1,1,8,8,256]{4,3,2,1,0:T(8,128)(2,1)S(1)} %get-tuple-element.5), channel_id=1, source_target_pairs={{0,2},{2,4},{4,6},{6,8},{8,10},{10,12},{12,14},{1,3},{3,5},{5,7},{... | collective-permute-start | bytes 98312 | tf_op jit(solution)/shard_map/ppermute | solution.py:15
  12.1 1.3 collective-permute-start.1
  13.7 4.2 %collective-permute-done.1 = bf16[1,1,8,8,256]{4,3,2,1,0:T(8,128)(2,1)S(1)} collective-permute-done((bf16[1,1,8,8,256]{4,3,2,1,0:T(8,128)(2,1)S(1)}, bf16[1,1,8,8,256]{4,3,2,1,0:T(8,128)(2,1)S(1)}, u32[]{:S(2)}, u32[]{:S(2)}) %collective-permute-start.1) | collective-permute-done | bytes 32800 | tf_op jit(solution)/shard_map/ppermute | solution.py:17
  19.0 34.5 %all-gather.2.cloned.1.call-done = bf16[256,27,256]{2,0,1:T(8,128)(2,1)} async-done(((bf16[16,27,256]{2,0,1:T(8,128)(2,1)}), bf16[256,27,256]{2,0,1:T(8,128)(2,1)}) %all-gather.2.cloned.1.call-update) | async-done | bytes 3538960 | tf_op jit(solution)/shard_map/all_gather | solution.py:125
  53.5 1.3 fusion.82
  54.8 1.1 fusion.81
  56.0 1.1 fusion.80
  57.1 1.1 convolution_add_fusion.47
  58.2 1.1 convolution_add_fusion.46
  59.4 1.1 convolution_add_fusion.45
  71.7 3.4 %broadcast_multiply_fusion = f32[256,27,256]{2,0,1:T(8,128)} fusion(f32[256,27,256]{2,0,1:T(8,128)S(1)} %fusion.4), kind=kLoop, calls=%fused_computation | loop fusion | flops 1769472 | bytes 14155776 | tf_op jit(solution)/shard_map/mul | solution.py:105
  75.2 3.6 %collective-permute-start.2 = (bf16[1,1,8,8,256]{4,3,2,1,0:T(8,128)(2,1)S(1)}, bf16[1,1,8,8,256]{4,3,2,1,0:T(8,128)(2,1)S(1)}, u32[]{:S(2)}, u32[]{:S(2)}) collective-permute-start(bf16[1,1,8,8,256]{4,3,2,1,0:T(8,128)(2,1)S(1)} %get-tuple-element.3), channel_id=1, source_target_pairs={{0,2},{2,4},{4,6},{6,8},{8,10},{10,12},{12,14},{1,3},{3,5},{5,7},{... | collective-permute-start | bytes 98312 | tf_op jit(solution)/shard_map/ppermute | solution.py:15
  78.8 1.3 collective-permute-start.3
  80.9 3.8 %collective-permute-done.3 = bf16[1,1,8,8,256]{4,3,2,1,0:T(8,128)(2,1)S(1)} collective-permute-done((bf16[1,1,8,8,256]{4,3,2,1,0:T(8,128)(2,1)S(1)}, bf16[1,1,8,8,256]{4,3,2,1,0:T(8,128)(2,1)S(1)}, u32[]{:S(2)}, u32[]{:S(2)}) %collective-permute-start.3) | collective-permute-done | bytes 32800 | tf_op jit(solution)/shard_map/ppermute | solution.py:17
  84.8 1.1 fusion.38
  85.9 1.1 fusion.42
  87.0 1.1 fusion.46
  88.1 1.1 convolution_add_fusion.23
  93.2 45.6 %reduce-scatter.2.cloned.1.call-done = f32[16,27,256]{2,0,1:T(8,128)} async-done(((f32[256,27,256]{2,0,1:T(8,128)}), f32[16,27,256]{2,0,1:T(8,128)}) %reduce-scatter.2.cloned.1.call-update) | async-done | bytes 442384 | tf_op jit(solution)/shard_map/reduce_scatter | solution.py:132
  138.9 1.1 convolution_add_fusion.2
  140.0 1.1 convolution_add_fusion.1
  141.1 1.8 fusion.32
  142.8 96.2 %all-reduce.4.cloned.1.call-done = f32[16,27,256]{2,0,1:T(8,128)} async-done(((f32[16,27,256]{2,0,1:T(8,128)}), f32[16,27,256]{2,0,1:T(8,128)}) %all-reduce.4.cloned.1.call-update) | async-done | bytes 442384 | tf_op jit(solution)/shard_map/psum | solution.py:133
  239.1 1.8 copy.87
  (89 shorter events, 18.6 us)
Async XLA Ops:
  7.2 53.3 %copy-start.2 = (bf16[1,4,8,8,256]{4,3,2,1,0:T(8,128)(2,1)S(1)}, bf16[1,4,8,8,256]{4,3,2,1,0:T(8,128)(2,1)}, u32[]{:S(2)}) copy-start(bf16[1,4,8,8,256]{4,3,2,1,0:T(8,128)(2,1)} %param.3) | copy-start | bytes 393220
  7.2 46.4 %all-gather.2.cloned.1.call-start = ((), (), s32[]{:S(2)}) async-start(), calls=%async_computation.1 | async-start | bytes 3760128 | tf_op jit(solution)/shard_map/all_gather | solution.py:125
  7.9 130.9 %reduce-scatter.2.cloned.1.call-start = ((), (), s32[]{:S(2)}) async-start(), calls=%async_computation.2 | async-start | bytes 7520256 | tf_op jit(solution)/shard_map/reduce_scatter | solution.py:132
  8.7 5.0 %collective-permute-start = (bf16[1,1,8,8,256]{4,3,2,1,0:T(8,128)(2,1)S(1)}, bf16[1,1,8,8,256]{4,3,2,1,0:T(8,128)(2,1)S(1)}, u32[]{:S(2)}, u32[]{:S(2)}) collective-permute-start(bf16[1,1,8,8,256]{4,3,2,1,0:T(8,128)(2,1)S(1)} %get-tuple-element.5), channel_id=1, source_target_pairs={{0,2},{2,4},{4,6},{6,8},{8,10},{10,12},{12,14},{1,3},{3,5},{5,7},{... | collective-permute-start | bytes 98312 | tf_op jit(solution)/shard_map/ppermute | solution.py:15
  12.1 5.8 %collective-permute-start.1 = (bf16[1,1,8,8,256]{4,3,2,1,0:T(8,128)(2,1)S(1)}, bf16[1,1,8,8,256]{4,3,2,1,0:T(8,128)(2,1)S(1)}, u32[]{:S(2)}, u32[]{:S(2)}) collective-permute-start(bf16[1,1,8,8,256]{4,3,2,1,0:T(8,128)(2,1)S(1)} %get-tuple-element.6), channel_id=1, source_target_pairs={{2,0},{4,2},{6,4},{8,6},{10,8},{12,10},{14,12},{3,1},{5,3},{7,5},{... | collective-permute-start | bytes 98312 | tf_op jit(solution)/shard_map/ppermute | solution.py:17
  53.5 7.0 %copy-start = (bf16[256,27,256]{2,0,1:T(8,128)(2,1)S(1)}, bf16[256,27,256]{2,0,1:T(8,128)(2,1)}, u32[]{:S(2)}) copy-start(bf16[256,27,256]{2,0,1:T(8,128)(2,1)} %all-gather.2.cloned.1.call-done) | copy-start | bytes 10616836
  63.1 2.1 copy-start.3
  75.1 163.9 %all-reduce.4.cloned.1.call-start = ((), (), s32[]{:S(2)}) async-start(), calls=%async_computation.3 | async-start | bytes 884736 | tf_op jit(solution)/shard_map/psum | solution.py:133
  75.2 14.1 %copy-start.1 = (bf16[256,27,256]{2,0,1:T(8,128)(2,1)S(1)}, bf16[256,27,256]{2,0,1:T(8,128)(2,1)}, u32[]{:S(2)}) copy-start(bf16[256,27,256]{2,0,1:T(8,128)(2,1)} %all-gather.2.cloned.1.call-done) | copy-start | bytes 10616836
  75.2 5.7 %collective-permute-start.2 = (bf16[1,1,8,8,256]{4,3,2,1,0:T(8,128)(2,1)S(1)}, bf16[1,1,8,8,256]{4,3,2,1,0:T(8,128)(2,1)S(1)}, u32[]{:S(2)}, u32[]{:S(2)}) collective-permute-start(bf16[1,1,8,8,256]{4,3,2,1,0:T(8,128)(2,1)S(1)} %get-tuple-element.3), channel_id=1, source_target_pairs={{0,2},{2,4},{4,6},{6,8},{8,10},{10,12},{12,14},{1,3},{3,5},{5,7},{... | collective-permute-start | bytes 98312 | tf_op jit(solution)/shard_map/ppermute | solution.py:15
  78.8 5.8 %collective-permute-start.3 = (bf16[1,1,8,8,256]{4,3,2,1,0:T(8,128)(2,1)S(1)}, bf16[1,1,8,8,256]{4,3,2,1,0:T(8,128)(2,1)S(1)}, u32[]{:S(2)}, u32[]{:S(2)}) collective-permute-start(bf16[1,1,8,8,256]{4,3,2,1,0:T(8,128)(2,1)S(1)} %get-tuple-element.4), channel_id=1, source_target_pairs={{2,0},{4,2},{6,4},{8,6},{10,8},{12,10},{14,12},{3,1},{5,3},{7,5},{... | collective-permute-start | bytes 98312 | tf_op jit(solution)/shard_map/ppermute | solution.py:17
Sparse Core Ops, SparseCore 0:
  9.9 43.6 all-gather.1
  75.2 63.5 reduce-scatter.1
  142.4 96.5 all-reduce.3
where the time goes:
time: 248 us; the launch traced here: 247 us
  waiting for transfers between devices  185 us (75%)
  matrix products  30 us (12%)
  between operations  14.4 us (6%)
  starting transfers between devices  9.72 us (4%)
  other arithmetic  5.36 us (2%)
  local copies, waits for them, and re-layouts  2.61 us (1%)
    psum x1, waiting for transfers between devices, local(): weight_grad = lax.psum(shard, ('slab', 'rep'))  96.2 us
    reduce_scatter x1, waiting for transfers between devices, local(): shard = lax.psum_scatter(terms, 'fsdp', scatter_dimension=0, tiled=True)  45.6 us
    all_gather x1, waiting for transfers between devices, local(): whole = lax.all_gather(weights, 'fsdp', axis=0, tiled=True)  34.5 us
    dot_general x27, matrix products, backward_rows(): jnp.einsum('bxyzo,oi->bxyzi', grad_window, weight_rows[:, index, :], pref...  12.2 us
    dot_general x27, matrix products, forward_rows(): jnp.einsum('bxyzi,oi->bxyzo', window, weight_rows[:, index, :], preferred...  11.7 us
    ppermute x2, waiting for transfers between devices, padded_2(): lax.ppermute(head, axis, [((i + 1) % count, i) for i in range(ends)])  8 us
    ppermute x2, starting transfers between devices, padded_2(): lax.ppermute(tail, axis, [(i, (i + 1) % count) for i in range(ends)])  7.02 us
    dot_general x27, matrix products, weight_terms(): jnp.einsum('bxyzo,bxyzi->oi', grads, window, preferred_element_type=jnp.f...  6.1 us
  transfers between devices with their start and end apart: 7, of which 6 were waited for; matrix products, arithmetic and copies ran while one was open for 6% of the time, Pallas kernels for 0%

commit v1 on v0

--- a/solution.py
+++ b/solution.py
@@ -122,7 +122,9 @@
     factor = float(total_cells) ** (-0.5)
     inputs_halo = padded_2(inputs, (("slab", 1),), 1)
     inputs_pad = pad_cross(inputs_halo)
-    whole = lax.all_gather(weights, "fsdp", axis=0, tiled=True)
+    whole = jnp.concatenate(
+        lax.all_to_all(jnp.stack([weights] * lax.axis_size("fsdp")), "fsdp", 0, 0), axis=0
+    )
     preact = forward_rows(inputs_pad, whole)
     activated = jax.nn.silu(preact).astype(jnp.bfloat16)
     grad_pre = (upstream.astype(jnp.float32) * silu_slope(preact)).astype(jnp.bfloat16)

time: 248 us -> 291 us (1.17)
  waiting for transfers between devices: 185 us -> 220 us
  starting transfers between devices: 9.72 us -> 18.2 us
  matrix products: 30 us -> 22.3 us
  local copies, waits for them, and re-layouts: 2.61 us -> 8.16 us
    all_to_all x0 -> x1, waiting for transfers between devices: none -> 68.1 us  [local(): lax.all_to_all(jnp.stack([weights] * lax.axis_size('fsdp')), 'fsdp', 0, 0)]
    all_gather x1 -> x0, waiting for transfers between devices: 34.5 us -> none  [local(): whole = lax.all_gather(weights, 'fsdp', axis=0, tiled=True)]
    all_to_all x0 -> x1, starting transfers between devices: none -> 8.72 us  [local(): lax.all_to_all(jnp.stack([weights] * lax.axis_size('fsdp')), 'fsdp', 0, 0)]
    dot_general x27, matrix products: 11.7 us -> 6.79 us  [forward_rows(): jnp.einsum('bxyzi,oi->bxyzo', window, weight_rows[:, index, :], preferred...]
    reduce_scatter x1, waiting for transfers between devices: 45.6 us -> 48.8 us  [local(): shard = lax.psum_scatter(terms, 'fsdp', scatter_dimension=0, tiled=True)]
    another operation x0 -> x1, local copies, waits for them, and re-layouts: none -> 2.97 us  [local(): jnp.stack([weights] * lax.axis_size('fsdp'))]
  transfers between devices with their start and end apart: 7 -> 7, of which waited for: 6 -> 6; matrix products, arithmetic and copies ran while one was open for 6% -> 5% of each run, Pallas kernels for 0% -> 0%
where the time goes in v1:
time: 291 us
  waiting for transfers between devices  220 us (76%)
  matrix products  22.3 us (8%)
  starting transfers between devices  18.2 us (6%)
  between operations  14.7 us (5%)
  local copies, waits for them, and re-layouts  8.16 us (3%)
  other arithmetic  7.06 us (2%)
    psum x1, waiting for transfers between devices, local(): weight_grad = lax.psum(shard, ('slab', 'rep'))  96 us
    all_to_all x1, waiting for transfers between devices, local(): lax.all_to_all(jnp.stack([weights] * lax.axis_size('fsdp')), 'fsdp', 0, 0)  68.1 us
    reduce_scatter x1, waiting for transfers between devices, local(): shard = lax.psum_scatter(terms, 'fsdp', scatter_dimension=0, tiled=True)  48.8 us
    dot_general x27, matrix products, backward_rows(): jnp.einsum('bxyzo,oi->bxyzi', grad_window, weight_rows[:, index, :], pref...  9.4 us
    all_to_all x1, starting transfers between devices, local(): lax.all_to_all(jnp.stack([weights] * lax.axis_size('fsdp')), 'fsdp', 0, 0)  8.72 us
    ppermute x2, waiting for transfers between devices, padded_2(): lax.ppermute(head, axis, [((i + 1) % count, i) for i in range(ends)])  7.05 us
    dot_general x27, matrix products, forward_rows(): jnp.einsum('bxyzi,oi->bxyzo', window, weight_rows[:, index, :], preferred...  6.79 us
    ppermute x2, starting transfers between devices, padded_2(): lax.ppermute(tail, axis, [(i, (i + 1) % count) for i in range(ends)])  6.78 us
  transfers between devices with their start and end apart: 7, of which 6 were waited for; matrix products, arithmetic and copies ran while one was open for 5% of the time, Pallas kernels for 0%

profile of v1, /device:TPU:32, one launch (start us, length us, event | category | flops | bytes accessed | tf_op | source)
XLA Modules:
  0.0 290.7 jit_solution(16517091899144934665)
XLA Ops:
  7.2 3.0 %stack.103 = bf16[16,16,27,256]{3,1,2,0:T(8,128)(2,1)} broadcast(bf16[16,27,256]{2,0,1:T(8,128)(2,1)} %param.4), dimensions={1,2,3} | broadcast | bytes 3760128 | tf_op jit(solution)/shard_map/stack | solution.py:126
  10.1 8.7 %all-to-all-start = ((bf16[16,16,27,256]{3,1,2,0:T(8,128)(2,1)}), bf16[16,16,27,256]{3,1,2,0:T(8,128)(2,1)}, u32[]{:S(2)}, u32[]{:S(2)}) async-start(bf16[16,16,27,256]{3,1,2,0:T(8,128)(2,1)} %stack.103), calls=%async_computation | async-start | bytes 7077888 | tf_op jit(solution)/shard_map/all_to_all | solution.py:126
  18.9 3.4 %collective-permute-start = (bf16[1,1,8,8,256]{4,3,2,1,0:T(8,128)(2,1)S(1)}, bf16[1,1,8,8,256]{4,3,2,1,0:T(8,128)(2,1)S(1)}, u32[]{:S(2)}, u32[]{:S(2)}) collective-permute-start(bf16[1,1,8,8,256]{4,3,2,1,0:T(8,128)(2,1)S(1)} %get-tuple-element.5), channel_id=1, source_target_pairs={{0,2},{2,4},{4,6},{6,8},{8,10},{10,12},{12,14},{1,3},{3,5},{5,7},{... | collective-permute-start | bytes 98312 | tf_op jit(solution)/shard_map/ppermute | solution.py:15
  22.3 1.3 collective-permute-start.1
  23.6 0.3 collective-permute-done
  23.9 4.2 %collective-permute-done.1 = bf16[1,1,8,8,256]{4,3,2,1,0:T(8,128)(2,1)S(1)} collective-permute-done((bf16[1,1,8,8,256]{4,3,2,1,0:T(8,128)(2,1)S(1)}, bf16[1,1,8,8,256]{4,3,2,1,0:T(8,128)(2,1)S(1)}, u32[]{:S(2)}, u32[]{:S(2)}) %collective-permute-start.1) | collective-permute-done | bytes 32800 | tf_op jit(solution)/shard_map/ppermute | solution.py:17
  28.1 1.0 select_maximum_fusion.2
  29.1 68.1 %all-to-all-done = bf16[16,16,27,256]{3,1,2,0:T(8,128)(2,1)} async-done(((bf16[16,16,27,256]{3,1,2,0:T(8,128)(2,1)}), bf16[16,16,27,256]{3,1,2,0:T(8,128)(2,1)}, u32[]{:S(2)}, u32[]{:S(2)}) %all-to-all-start) | async-done | bytes 3538976 | tf_op jit(solution)/shard_map/all_to_all | solution.py:126
  97.2 2.5 copy.6
  105.9 1.0 fusion.37
  113.1 3.3 %broadcast_multiply_fusion = f32[256,27,256]{2,0,1:T(8,128)} fusion(f32[256,27,256]{2,0,1:T(8,128)S(1)} %fusion.4), kind=kLoop, calls=%fused_computation | loop fusion | flops 1769472 | bytes 14155776 | tf_op jit(solution)/shard_map/mul | solution.py:105
  116.5 0.8 fusion.93
  117.4 3.4 %collective-permute-start.2 = (bf16[1,1,8,8,256]{4,3,2,1,0:T(8,128)(2,1)S(1)}, bf16[1,1,8,8,256]{4,3,2,1,0:T(8,128)(2,1)S(1)}, u32[]{:S(2)}, u32[]{:S(2)}) collective-permute-start(bf16[1,1,8,8,256]{4,3,2,1,0:T(8,128)(2,1)S(1)} %get-tuple-element.3), channel_id=1, source_target_pairs={{0,2},{2,4},{4,6},{6,8},{8,10},{10,12},{12,14},{1,3},{3,5},{5,7},{... | collective-permute-start | bytes 98312 | tf_op jit(solution)/shard_map/ppermute | solution.py:15
  120.8 1.3 collective-permute-start.3
  122.1 1.7 fusion.79
  123.7 2.8 collective-permute-done.3
  126.6 1.1 select_maximum_fusion
  132.2 0.9 fusion
  133.1 48.8 %reduce-scatter.2.cloned.1.call-done = f32[16,27,256]{2,0,1:T(8,128)} async-done(((f32[256,27,256]{2,0,1:T(8,128)}), f32[16,27,256]{2,0,1:T(8,128)}) %reduce-scatter.2.cloned.1.call-update) | async-done | bytes 442384 | tf_op jit(solution)/shard_map/reduce_scatter | solution.py:134
  181.9 1.2 convolution_add_fusion.2
  183.2 1.1 convolution_add_fusion.1
  184.3 1.8 fusion.32
  186.1 96.0 %all-reduce.4.cloned.1.call-done = f32[16,27,256]{2,0,1:T(8,128)} async-done(((f32[16,27,256]{2,0,1:T(8,128)}), f32[16,27,256]{2,0,1:T(8,128)}) %all-reduce.4.cloned.1.call-update) | async-done | bytes 442384 | tf_op jit(solution)/shard_map/psum | solution.py:135
  282.1 1.8 copy.88
  (104 shorter events, 16.5 us)
Async XLA Ops:
  10.1 8.8 %copy-start.2 = (bf16[1,4,8,8,256]{4,3,2,1,0:T(8,128)(2,1)S(1)}, bf16[1,4,8,8,256]{4,3,2,1,0:T(8,128)(2,1)}, u32[]{:S(2)}) copy-start(bf16[1,4,8,8,256]{4,3,2,1,0:T(8,128)(2,1)} %param.3) | copy-start | bytes 393220
  10.1 87.1 %all-to-all-start = ((bf16[16,16,27,256]{3,1,2,0:T(8,128)(2,1)}), bf16[16,16,27,256]{3,1,2,0:T(8,128)(2,1)}, u32[]{:S(2)}, u32[]{:S(2)}) async-start(bf16[16,16,27,256]{3,1,2,0:T(8,128)(2,1)} %stack.103), calls=%async_computation | async-start | bytes 7077888 | tf_op jit(solution)/shard_map/all_to_all | solution.py:126
  18.9 163.1 %reduce-scatter.2.cloned.1.call-start = ((), (), s32[]{:S(2)}) async-start(), calls=%async_computation.2 | async-start | bytes 7520256 | tf_op jit(solution)/shard_map/reduce_scatter | solution.py:134
  18.9 5.0 %collective-permute-start = (bf16[1,1,8,8,256]{4,3,2,1,0:T(8,128)(2,1)S(1)}, bf16[1,1,8,8,256]{4,3,2,1,0:T(8,128)(2,1)S(1)}, u32[]{:S(2)}, u32[]{:S(2)}) collective-permute-start(bf16[1,1,8,8,256]{4,3,2,1,0:T(8,128)(2,1)S(1)} %get-tuple-element.5), channel_id=1, source_target_pairs={{0,2},{2,4},{4,6},{6,8},{8,10},{10,12},{12,14},{1,3},{3,5},{5,7},{... | collective-permute-start | bytes 98312 | tf_op jit(solution)/shard_map/ppermute | solution.py:15
  22.3 5.8 %collective-permute-start.1 = (bf16[1,1,8,8,256]{4,3,2,1,0:T(8,128)(2,1)S(1)}, bf16[1,1,8,8,256]{4,3,2,1,0:T(8,128)(2,1)S(1)}, u32[]{:S(2)}, u32[]{:S(2)}) collective-permute-start(bf16[1,1,8,8,256]{4,3,2,1,0:T(8,128)(2,1)S(1)} %get-tuple-element.6), channel_id=1, source_target_pairs={{2,0},{4,2},{6,4},{8,6},{10,8},{12,10},{14,12},{3,1},{5,3},{7,5},{... | collective-permute-start | bytes 98312 | tf_op jit(solution)/shard_map/ppermute | solution.py:17
  23.9 5.2 %copy-start.8 = (bf16[1,1,8,8,256]{4,3,2,1,0:T(8,128)(2,1)}, bf16[1,1,8,8,256]{4,3,2,1,0:T(8,128)(2,1)S(1)}, u32[]{:S(2)}) copy-start(bf16[1,1,8,8,256]{4,3,2,1,0:T(8,128)(2,1)S(1)} %collective-permute-done) | copy-start | bytes 98308
  28.1 1.0 copy-start.6
  97.2 2.5 copy-start.1
  99.8 1.4 copy-start.3
  99.8 1.4 copy-start.9
  103.0 2.1 copy-start.7
  103.8 2.1 copy-start.10
  106.8 6.0 %copy-start.4 = (bf16[1,4,8,8,256]{4,3,2,1,0:T(8,128)(2,1)}, bf16[1,4,8,8,256]{4,3,2,1,0:T(8,128)(2,1)S(1)}, u32[]{:S(2)}) copy-start(bf16[1,4,8,8,256]{4,3,2,1,0:T(8,128)(2,1)S(1)} %get-tuple-element.7) | copy-start | bytes 393220
  116.5 165.6 %all-reduce.4.cloned.1.call-start = ((), (), s32[]{:S(2)}) async-start(), calls=%async_computation.3 | async-start | bytes 884736 | tf_op jit(solution)/shard_map/psum | solution.py:135
  116.5 12.3 %copy-start.5 = (bf16[1,4,8,8,256]{4,3,2,1,0:T(8,128)(2,1)S(1)}, bf16[1,4,8,8,256]{4,3,2,1,0:T(8,128)(2,1)}, u32[]{:S(2)}) copy-start(bf16[1,4,8,8,256]{4,3,2,1,0:T(8,128)(2,1)} %copy-done.4) | copy-start | bytes 393220
  117.4 6.4 %collective-permute-start.2 = (bf16[1,1,8,8,256]{4,3,2,1,0:T(8,128)(2,1)S(1)}, bf16[1,1,8,8,256]{4,3,2,1,0:T(8,128)(2,1)S(1)}, u32[]{:S(2)}, u32[]{:S(2)}) collective-permute-start(bf16[1,1,8,8,256]{4,3,2,1,0:T(8,128)(2,1)S(1)} %get-tuple-element.3), channel_id=1, source_target_pairs={{0,2},{2,4},{4,6},{6,8},{8,10},{10,12},{12,14},{1,3},{3,5},{5,7},{... | collective-permute-start | bytes 98312 | tf_op jit(solution)/shard_map/ppermute | solution.py:15
  120.8 5.8 %collective-permute-start.3 = (bf16[1,1,8,8,256]{4,3,2,1,0:T(8,128)(2,1)S(1)}, bf16[1,1,8,8,256]{4,3,2,1,0:T(8,128)(2,1)S(1)}, u32[]{:S(2)}, u32[]{:S(2)}) collective-permute-start(bf16[1,1,8,8,256]{4,3,2,1,0:T(8,128)(2,1)S(1)} %get-tuple-element.4), channel_id=1, source_target_pairs={{2,0},{4,2},{6,4},{8,6},{10,8},{12,10},{14,12},{3,1},{5,3},{7,5},{... | collective-permute-start | bytes 98312 | tf_op jit(solution)/shard_map/ppermute | solution.py:17
  127.6 4.4 %copy-start = (bf16[1,6,10,10,256]{4,3,2,1,0:T(8,128)(2,1)}, bf16[1,6,10,10,256]{4,3,2,1,0:T(8,128)(2,1)S(1)}, u32[]{:S(2)}) copy-start(bf16[1,6,10,10,256]{4,3,2,1,0:T(8,128)(2,1)S(1)} %select_maximum_fusion) | copy-start | bytes 921604
Sparse Core Ops, SparseCore 0:
  116.6 65.2 reduce-scatter.1
  185.5 96.5 all-reduce.3
